TPU v7x, 512 devices: a whole 4x4x16 slice. The times are simulated.
512 devices in a mesh: region: 16 (over y, x), member: 32 (over z, core).
Axes of the slice: x: 4, y: 4, z: 16, core: 2. Of those that a mesh axis runs over, the one named last changes fastest.
Arguments:
- sample_matrix: bfloat16 [128, 1048576], P('member', 'region'), may hold values from -6 to 6
- state_coords: float32 [3, 1048576], P(None, ('region', 'member')), may hold values from 0 to 1
- obs_model: bfloat16 [128, 16384], P('member', 'region'), may hold values from -6 to 6
- innovations: bfloat16 [128, 16384], P('member', 'region'), may hold values from -6 to 6
- obs_error: float32 [16384], P('region'), may hold values from 0.25 to 4
- obs_coords: float32 [3, 16384], P(None, 'region'), may hold values from 0 to 1
- neighbours: int32 [16, 2], P('region'), may hold values from 0 to 15, as said below
- pattern: int32 [8192, 12], P(('region', 'member')), may hold values from 0 to 23
- counts: int32 [8192], P(('region', 'member')), may hold values from 1 to 12
Outputs:
- analysis: bfloat16 [128, 1048576], P('member', 'region')
Inputs may be any that keep to these rules, and one draw needn't show every extreme that they name: `neighbours`: two distinct regions, both other than the region itself.
All inputs are finite; a program needn't handle non-finite values.
Results may differ from a plain program's by a relative error of at most 0.011.
Values may be sent and summed in bfloat16 or wider, within the bound.
A program may use at most 64 MiB of HBM per device.

v0:
```python
import jax
import jax.numpy as jnp
from jax import lax
from jax.sharding import PartitionSpec as P

half_width = 0.6


def gaspari(distance):
    scaled = distance / half_width
    near_part = (
        ((-0.25 * scaled + 0.5) * scaled + 0.625) * scaled - 5.0 / 3.0
    ) * scaled * scaled + 1.0
    clipped = jnp.maximum(scaled, 1.0)
    far_part = (
        ((((scaled / 12.0 - 0.5) * scaled + 0.625) * scaled + 5.0 / 3.0) * scaled - 5.0) * scaled
        + 4.0
        - 2.0 / (3.0 * clipped)
    )
    return jnp.where(scaled <= 1.0, near_part, jnp.where(scaled <= 2.0, far_part, 0.0))


def prepare(model_rows, innov_rows, error_row):
    sample_collection = model_rows.shape[0]
    model_float = model_rows.astype(jnp.float32)
    obs_dev = model_float - jnp.sum(model_float, axis=0) / sample_collection
    spread = jnp.sum(obs_dev * obs_dev, axis=0) / (sample_collection - 1) + error_row
    return (
        obs_dev.astype(jnp.bfloat16),
        (innov_rows.astype(jnp.float32) / spread).astype(jnp.bfloat16),
    )


def pick_regions(array, chosen, regions_all):
    leading = array.shape[0]
    split = array.reshape(leading, regions_all, -1)
    return jnp.take(split, chosen, axis=1).reshape(leading, -1)


def on_device(
    sample_matrix,
    state_coords,
    obs_model,
    innovations,
    obs_error,
    obs_coords,
    neighbours,
    pattern,
    counts,
):
    regrouped = lax.all_to_all(sample_matrix, "member", split_axis=1, concat_axis=0, tiled=True)
    sample_collection = regrouped.shape[0]
    blocks = pattern.shape[0]
    slots_all = pattern.shape[1]
    block_width = regrouped.shape[1] // blocks
    state_float = regrouped.astype(jnp.float32)
    centre = jnp.sum(state_float, axis=0) / sample_collection
    state_anom = (
        (state_float - centre).astype(jnp.bfloat16).reshape(sample_collection, blocks, block_width)
    )
    state_xyz = state_coords.reshape(3, blocks, block_width)
    regions_all = lax.axis_size("region")
    own_region = lax.axis_index("region")
    chosen = jnp.concatenate([own_region.reshape(1), neighbours.reshape(-1)])
    full_model, full_innov = (
        lax.all_gather(obs_model, "member", axis=0, tiled=True),
        lax.all_gather(innovations, "member", axis=0, tiled=True),
    )
    obs_anom, weighted = prepare(full_model, full_innov, obs_error)
    every_anom, every_weight, every_xyz = (
        lax.all_gather(obs_anom, "region", axis=1, tiled=True),
        lax.all_gather(weighted, "region", axis=1, tiled=True),
        lax.all_gather(obs_coords.astype(jnp.bfloat16), "region", axis=1, tiled=True).astype(
            obs_coords.dtype
        ),
    )
    panel_anom = pick_regions(every_anom, chosen, regions_all)
    panel_weight = pick_regions(every_weight, chosen, regions_all)
    panel_xyz = pick_regions(every_xyz, chosen, regions_all)
    panel_anom = panel_anom.reshape(sample_collection, -1, block_width)
    panel_weight = panel_weight.reshape(sample_collection, -1, block_width)
    panel_xyz = panel_xyz.reshape(3, -1, block_width)

    def slot_term(slot_index, update_shift):
        slot_ids = pattern[:, slot_index]
        live_mask = (counts > slot_index).astype(jnp.float32)
        obs_part = jnp.take(panel_anom, slot_ids, axis=1)
        obs_weight = jnp.take(panel_weight, slot_ids, axis=1)
        obs_pos = jnp.take(panel_xyz, slot_ids, axis=1)
        covariance = jnp.einsum(
            "mbe,mbo->beo", state_anom, obs_part, preferred_element_type=jnp.float32
        ) / (sample_collection - 1)
        offset = state_xyz[:, :, :, None] - obs_pos[:, :, None, :]
        distance = jnp.sqrt(offset[0] * offset[0] + offset[1] * offset[1] + offset[2] * offset[2])
        gain_block = (gaspari(distance) * covariance * live_mask[:, None, None]).astype(
            jnp.bfloat16
        )
        return update_shift + jnp.einsum(
            "mbo,beo->mbe", obs_weight, gain_block, preferred_element_type=jnp.float32
        )

    starting = jnp.zeros((sample_collection, blocks, block_width), jnp.float32)
    update_shift = lax.fori_loop(0, slots_all, slot_term, starting)
    updated = (state_float + update_shift.reshape(sample_collection, -1)).astype(jnp.bfloat16)
    return lax.all_to_all(updated, "member", split_axis=0, concat_axis=1, tiled=True)


def solution(mesh):
    in_specs = (
        P("member", "region"),
        P(None, ("region", "member")),
        P("member", "region"),
        P("member", "region"),
        P("region"),
        P(None, "region"),
        P("region", None),
        P(("region", "member"), None),
        P(("region", "member")),
    )
    out_specs = P("member", "region")
    return jax.shard_map(
        on_device, mesh=mesh, in_specs=in_specs, out_specs=out_specs, check_vma=False
    )
```

profile of v0, /device:TPU:1, one launch (start us, length us, event | category | flops | bytes accessed | tf_op | source)
XLA Modules:
  0.0 426.2 jit_solution(7567697888767191045)
XLA Ops:
  6.5 38.7 %all-gather = bf16[32,4,1024]{2,1,0:T(4,128)(2,1)S(1)} all-gather(bf16[1,4,1024]{2,1,0:T(4,128)(2,1)} %bitcast.156), channel_id=1, replica_groups=mesh['region'=16,'member'=32] {'member'}, dimensions={0}, use_global_device_ids=true | all-gather | bytes 270336 | tf_op jit(solution)/shard_map/all_gather | solution.py:66
  45.4 28.1 %all-gather.1 = bf16[32,4,1024]{2,1,0:T(4,128)(2,1)S(1)} all-gather(bf16[1,4,1024]{2,1,0:T(4,128)(2,1)} %bitcast.157), channel_id=1, replica_groups=mesh['region'=16,'member'=32] {'member'}, dimensions={0}, use_global_device_ids=true | all-gather | bytes 270336 | tf_op jit(solution)/shard_map/all_gather | solution.py:67
  76.5 7.6 %all-to-all-start = ((bf16[4,32,2048]{2,0,1:T(4,128)(2,1)}), bf16[4,32,2048]{2,0,1:T(4,128)(2,1)S(1)}, u32[]{:S(2)}, u32[]{:S(2)}) async-start(bf16[4,32,2048]{2,0,1:T(4,128)(2,1)} %bitcast), calls=%async_computation | async-start | bytes 1048576 | tf_op jit(solution)/shard_map/all_to_all | solution.py:51
  84.4 20.3 %all_gather.15 = bf16[3,16384]{1,0:T(4,128)(2,1)S(1)} all-gather(bf16[3,1024]{1,0:T(4,128)(2,1)S(1)} %convert_element_type.67), channel_id=1, replica_groups=mesh['region'=16,'member'=32] {'region'}, dimensions={1}, use_global_device_ids=true | all-gather | bytes 104448 | tf_op jit(solution)/shard_map/all_gather | solution.py:73
  105.6 12.0 %all-to-all-done = bf16[4,32,2048]{2,0,1:T(4,128)(2,1)S(1)} async-done(((bf16[4,32,2048]{2,0,1:T(4,128)(2,1)}), bf16[4,32,2048]{2,0,1:T(4,128)(2,1)S(1)}, u32[]{:S(2)}, u32[]{:S(2)}) %all-to-all-start) | async-done | bytes 524320 | tf_op jit(solution)/shard_map/all_to_all | solution.py:51
  118.5 1.2 fusion.77
  119.7 19.3 %all-gather.7.cloned.1.call-done = bf16[128,16384]{1,0:T(8,128)(2,1)} async-done(((bf16[128,1024]{1,0:T(8,128)(2,1)}), bf16[128,16384]{1,0:T(8,128)(2,1)}) %all-gather.7.cloned.1.call-update) | async-done | bytes 4194320 | tf_op jit(solution)/shard_map/all_gather | solution.py:72
  139.0 6.4 %copy.56 = bf16[128,16384]{0,1:T(8,128)(2,1)} copy(bf16[128,16384]{1,0:T(8,128)(2,1)} %all-gather.7.cloned.1.call-done) | data formatting | bytes 8388608 | tf_op jit(solution)/shard_map/all_gather | solution.py:72
  145.3 6.4 %copy.57 = bf16[128,16,1024]{2,0,1:T(8,128)(2,1)} copy(bf16[128,16,1024]{0,2,1:T(8,128)(2,1)} %bitcast.146) | data formatting | bytes 8388608 | tf_op jit(solution)/shard_map/reshape | solution.py:36
  151.8 56.9 %all-gather.5.cloned.1.call-done = bf16[128,16384]{1,0:T(8,128)(2,1)} async-done(((bf16[128,1024]{1,0:T(8,128)(2,1)}), bf16[128,16384]{1,0:T(8,128)(2,1)}) %all-gather.5.cloned.1.call-update) | async-done | bytes 4194320 | tf_op jit(solution)/shard_map/all_gather | solution.py:71
  208.7 6.4 %copy.52 = bf16[128,16384]{0,1:T(8,128)(2,1)} copy(bf16[128,16384]{1,0:T(8,128)(2,1)} %all-gather.5.cloned.1.call-done) | data formatting | bytes 8388608 | tf_op jit(solution)/shard_map/all_gather | solution.py:71
  215.1 6.4 %copy.53 = bf16[128,16,1024]{2,0,1:T(8,128)(2,1)} copy(bf16[128,16,1024]{0,2,1:T(8,128)(2,1)} %bitcast.147) | data formatting | bytes 8388608 | tf_op jit(solution)/shard_map/reshape | solution.py:36
  221.5 2.8 gather_fusion.5
  224.3 2.8 gather_fusion.4
  227.7 1.2 copy.60
  229.2 1.2 copy.61
  230.4 139.4 %while.16 = (s32[]{:T(128)}, f32[128,16,128]{0,2,1:T(8,128)}, f32[3,2048]{1,0:T(4,128)S(1)}, s32[16,12]{0,1:T(8,128)S(1)}, f32[3,24,128]{2,0,1:T(4,128)S(1)}, /*...) while((s32[]{:T(128)}, f32[128,16,128]{0,2,1:T(8,128)}, ...), condition=%wide.region_4.0_spmd.clone, body=%wide.region_3.6_spmd.clone.sunk | while | flops 145760480 | bytes 12316011 | solution.py:103
  231.2 0.9 broadcast_subtract_fusion.2
  232.1 2.6 gather_fusion.1
  234.6 2.6 gather_fusion.2
  237.2 4.5 %fusion.87 = f32[128,16,128]{0,2,1:T(8,128)} fusion(bf16[128,16,128]{2,0,1:T(8,128)(2,1)} %get-tuple-element.429, f32[128,16,128]{0,2,1:T(8,128)} %get-tuple-element.413, f32[3,16,128,128]{2,3,1,0:T(8,128)S(1)} %broadcast_subtract_fusion.2, bf16[16,128,128]{2,1,0:T(8,128)(2,1)} %gather_fusion.1, bf16[16,128,128]{2,1,0:T(8,128)(2,1)} %gather_fusion.2, ...), kind=kOutput, calls=%fused_computation.9.clone.1 | convolution fusion | flops 144965632 | bytes 6817281 | tf_op jit(solution)/shard_map/while/body/eval_jaxpr/mbo,beo->mbe/dot_general | solution.py:98
  242.5 0.9 broadcast_subtract_fusion.2
  243.4 2.6 gather_fusion.1
  245.9 2.6 gather_fusion.2
  248.5 4.9 %fusion.87 = f32[128,16,128]{0,2,1:T(8,128)} fusion(bf16[128,16,128]{2,0,1:T(8,128)(2,1)} %get-tuple-element.429, f32[128,16,128]{0,2,1:T(8,128)} %get-tuple-element.413, f32[3,16,128,128]{2,3,1,0:T(8,128)S(1)} %broadcast_subtract_fusion.2, bf16[16,128,128]{2,1,0:T(8,128)(2,1)} %gather_fusion.1, bf16[16,128,128]{2,1,0:T(8,128)(2,1)} %gather_fusion.2, ...), kind=kOutput, calls=%fused_computation.9.clone.1 | convolution fusion | flops 144965632 | bytes 6817281 | tf_op jit(solution)/shard_map/while/body/eval_jaxpr/mbo,beo->mbe/dot_general | solution.py:98
  254.1 0.9 broadcast_subtract_fusion.2
  255.0 2.6 gather_fusion.1
  257.6 2.6 gather_fusion.2
  260.1 4.9 %fusion.87 = f32[128,16,128]{0,2,1:T(8,128)} fusion(bf16[128,16,128]{2,0,1:T(8,128)(2,1)} %get-tuple-element.429, f32[128,16,128]{0,2,1:T(8,128)} %get-tuple-element.413, f32[3,16,128,128]{2,3,1,0:T(8,128)S(1)} %broadcast_subtract_fusion.2, bf16[16,128,128]{2,1,0:T(8,128)(2,1)} %gather_fusion.1, bf16[16,128,128]{2,1,0:T(8,128)(2,1)} %gather_fusion.2, ...), kind=kOutput, calls=%fused_computation.9.clone.1 | convolution fusion | flops 144965632 | bytes 6817281 | tf_op jit(solution)/shard_map/while/body/eval_jaxpr/mbo,beo->mbe/dot_general | solution.py:98
  265.7 0.9 broadcast_subtract_fusion.2
  266.7 2.6 gather_fusion.1
  269.2 2.6 gather_fusion.2
  271.8 4.9 %fusion.87 = f32[128,16,128]{0,2,1:T(8,128)} fusion(bf16[128,16,128]{2,0,1:T(8,128)(2,1)} %get-tuple-element.429, f32[128,16,128]{0,2,1:T(8,128)} %get-tuple-element.413, f32[3,16,128,128]{2,3,1,0:T(8,128)S(1)} %broadcast_subtract_fusion.2, bf16[16,128,128]{2,1,0:T(8,128)(2,1)} %gather_fusion.1, bf16[16,128,128]{2,1,0:T(8,128)(2,1)} %gather_fusion.2, ...), kind=kOutput, calls=%fused_computation.9.clone.1 | convolution fusion | flops 144965632 | bytes 6817281 | tf_op jit(solution)/shard_map/while/body/eval_jaxpr/mbo,beo->mbe/dot_general | solution.py:98
  277.4 0.9 broadcast_subtract_fusion.2
  278.3 2.6 gather_fusion.1
  280.9 2.6 gather_fusion.2
  283.4 4.9 %fusion.87 = f32[128,16,128]{0,2,1:T(8,128)} fusion(bf16[128,16,128]{2,0,1:T(8,128)(2,1)} %get-tuple-element.429, f32[128,16,128]{0,2,1:T(8,128)} %get-tuple-element.413, f32[3,16,128,128]{2,3,1,0:T(8,128)S(1)} %broadcast_subtract_fusion.2, bf16[16,128,128]{2,1,0:T(8,128)(2,1)} %gather_fusion.1, bf16[16,128,128]{2,1,0:T(8,128)(2,1)} %gather_fusion.2, ...), kind=kOutput, calls=%fused_computation.9.clone.1 | convolution fusion | flops 144965632 | bytes 6817281 | tf_op jit(solution)/shard_map/while/body/eval_jaxpr/mbo,beo->mbe/dot_general | solution.py:98
  289.0 0.9 broadcast_subtract_fusion.2
  289.9 2.6 gather_fusion.1
  292.5 2.6 gather_fusion.2
  295.1 4.9 %fusion.87 = f32[128,16,128]{0,2,1:T(8,128)} fusion(bf16[128,16,128]{2,0,1:T(8,128)(2,1)} %get-tuple-element.429, f32[128,16,128]{0,2,1:T(8,128)} %get-tuple-element.413, f32[3,16,128,128]{2,3,1,0:T(8,128)S(1)} %broadcast_subtract_fusion.2, bf16[16,128,128]{2,1,0:T(8,128)(2,1)} %gather_fusion.1, bf16[16,128,128]{2,1,0:T(8,128)(2,1)} %gather_fusion.2, ...), kind=kOutput, calls=%fused_computation.9.clone.1 | convolution fusion | flops 144965632 | bytes 6817281 | tf_op jit(solution)/shard_map/while/body/eval_jaxpr/mbo,beo->mbe/dot_general | solution.py:98
  300.7 0.9 broadcast_subtract_fusion.2
  301.6 2.6 gather_fusion.1
  304.1 2.6 gather_fusion.2
  306.7 4.9 %fusion.87 = f32[128,16,128]{0,2,1:T(8,128)} fusion(bf16[128,16,128]{2,0,1:T(8,128)(2,1)} %get-tuple-element.429, f32[128,16,128]{0,2,1:T(8,128)} %get-tuple-element.413, f32[3,16,128,128]{2,3,1,0:T(8,128)S(1)} %broadcast_subtract_fusion.2, bf16[16,128,128]{2,1,0:T(8,128)(2,1)} %gather_fusion.1, bf16[16,128,128]{2,1,0:T(8,128)(2,1)} %gather_fusion.2, ...), kind=kOutput, calls=%fused_computation.9.clone.1 | convolution fusion | flops 144965632 | bytes 6817281 | tf_op jit(solution)/shard_map/while/body/eval_jaxpr/mbo,beo->mbe/dot_general | solution.py:98
  312.3 0.9 broadcast_subtract_fusion.2
  313.2 2.6 gather_fusion.1
  315.8 2.6 gather_fusion.2
  318.3 4.9 %fusion.87 = f32[128,16,128]{0,2,1:T(8,128)} fusion(bf16[128,16,128]{2,0,1:T(8,128)(2,1)} %get-tuple-element.429, f32[128,16,128]{0,2,1:T(8,128)} %get-tuple-element.413, f32[3,16,128,128]{2,3,1,0:T(8,128)S(1)} %broadcast_subtract_fusion.2, bf16[16,128,128]{2,1,0:T(8,128)(2,1)} %gather_fusion.1, bf16[16,128,128]{2,1,0:T(8,128)(2,1)} %gather_fusion.2, ...), kind=kOutput, calls=%fused_computation.9.clone.1 | convolution fusion | flops 144965632 | bytes 6817281 | tf_op jit(solution)/shard_map/while/body/eval_jaxpr/mbo,beo->mbe/dot_general | solution.py:98
  324.9 2.6 gather_fusion.1
  327.4 2.6 gather_fusion.2
  330.0 4.9 %fusion.87 = f32[128,16,128]{0,2,1:T(8,128)} fusion(bf16[128,16,128]{2,0,1:T(8,128)(2,1)} %get-tuple-element.429, f32[128,16,128]{0,2,1:T(8,128)} %get-tuple-element.413, f32[3,16,128,128]{2,3,1,0:T(8,128)S(1)} %broadcast_subtract_fusion.2, bf16[16,128,128]{2,1,0:T(8,128)(2,1)} %gather_fusion.1, bf16[16,128,128]{2,1,0:T(8,128)(2,1)} %gather_fusion.2, ...), kind=kOutput, calls=%fused_computation.9.clone.1 | convolution fusion | flops 144965632 | bytes 6817281 | tf_op jit(solution)/shard_map/while/body/eval_jaxpr/mbo,beo->mbe/dot_general | solution.py:98
  336.5 2.6 gather_fusion.1
  339.1 2.6 gather_fusion.2
  341.6 4.9 %fusion.87 = f32[128,16,128]{0,2,1:T(8,128)} fusion(bf16[128,16,128]{2,0,1:T(8,128)(2,1)} %get-tuple-element.429, f32[128,16,128]{0,2,1:T(8,128)} %get-tuple-element.413, f32[3,16,128,128]{2,3,1,0:T(8,128)S(1)} %broadcast_subtract_fusion.2, bf16[16,128,128]{2,1,0:T(8,128)(2,1)} %gather_fusion.1, bf16[16,128,128]{2,1,0:T(8,128)(2,1)} %gather_fusion.2, ...), kind=kOutput, calls=%fused_computation.9.clone.1 | convolution fusion | flops 144965632 | bytes 6817281 | tf_op jit(solution)/shard_map/while/body/eval_jaxpr/mbo,beo->mbe/dot_general | solution.py:98
  348.2 2.6 gather_fusion.1
  350.7 2.6 gather_fusion.2
  353.3 4.9 %fusion.87 = f32[128,16,128]{0,2,1:T(8,128)} fusion(bf16[128,16,128]{2,0,1:T(8,128)(2,1)} %get-tuple-element.429, f32[128,16,128]{0,2,1:T(8,128)} %get-tuple-element.413, f32[3,16,128,128]{2,3,1,0:T(8,128)S(1)} %broadcast_subtract_fusion.2, bf16[16,128,128]{2,1,0:T(8,128)(2,1)} %gather_fusion.1, bf16[16,128,128]{2,1,0:T(8,128)(2,1)} %gather_fusion.2, ...), kind=kOutput, calls=%fused_computation.9.clone.1 | convolution fusion | flops 144965632 | bytes 6817281 | tf_op jit(solution)/shard_map/while/body/eval_jaxpr/mbo,beo->mbe/dot_general | solution.py:98
  358.9 0.9 broadcast_subtract_fusion.2
  359.8 2.6 gather_fusion.1
  362.3 2.6 gather_fusion.2
  364.9 4.9 %fusion.87 = f32[128,16,128]{0,2,1:T(8,128)} fusion(bf16[128,16,128]{2,0,1:T(8,128)(2,1)} %get-tuple-element.429, f32[128,16,128]{0,2,1:T(8,128)} %get-tuple-element.413, f32[3,16,128,128]{2,3,1,0:T(8,128)S(1)} %broadcast_subtract_fusion.2, bf16[16,128,128]{2,1,0:T(8,128)(2,1)} %gather_fusion.1, bf16[16,128,128]{2,1,0:T(8,128)(2,1)} %gather_fusion.2, ...), kind=kOutput, calls=%fused_computation.9.clone.1 | convolution fusion | flops 144965632 | bytes 6817281 | tf_op jit(solution)/shard_map/while/body/eval_jaxpr/mbo,beo->mbe/dot_general | solution.py:98
  369.8 1.8 copy.62
  372.3 46.3 %all_to_all.29 = bf16[32,4,2048]{2,1,0:T(4,128)(2,1)S(1)} all-to-all(bf16[32,4,2048]{2,1,0:T(4,128)(2,1)S(1)} %add_convert_fusion), channel_id=1, replica_groups=mesh['region'=16,'member'=32] {'member'}, dimensions={0} | all-to-all | bytes 1048576 | tf_op jit(solution)/shard_map/all_to_all | solution.py:105
  (146 shorter events, 18.9 us)
Async XLA Ops:
  6.5 77.6 %copy-start.6 = (s32[1,2]{1,0:T(1,128)S(1)}, s32[1,2]{1,0:T(1,128)}, u32[]{:S(2)}) copy-start(s32[1,2]{1,0:T(1,128)} %param.21) | copy-start | bytes 28
  6.5 77.8 %copy-start.3 = (f32[3,1024]{1,0:T(4,128)S(1)}, f32[3,1024]{1,0:T(4,128)}, u32[]{:S(2)}) copy-start(f32[3,1024]{1,0:T(4,128)} %param.20) | copy-start | bytes 36868
  6.5 98.2 %copy-start.5 = (s32[16,12]{1,0:T(8,128)S(1)}, s32[16,12]{1,0:T(8,128)}, u32[]{:S(2)}) copy-start(s32[16,12]{1,0:T(8,128)} %param.22) | copy-start | bytes 2308
  6.5 132.4 %all-gather.7.cloned.1.call-start = ((), (), s32[]{:S(2)}) async-start(), calls=%async_computation.3 | async-start | bytes 4456448 | tf_op jit(solution)/shard_map/all_gather | solution.py:72
  75.8 132.9 %all-gather.5.cloned.1.call-start = ((), (), s32[]{:S(2)}) async-start(), calls=%async_computation.2 | async-start | bytes 4456448 | tf_op jit(solution)/shard_map/all_gather | solution.py:71
  76.5 41.1 %all-to-all-start = ((bf16[4,32,2048]{2,0,1:T(4,128)(2,1)}), bf16[4,32,2048]{2,0,1:T(4,128)(2,1)S(1)}, u32[]{:S(2)}, u32[]{:S(2)}) async-start(bf16[4,32,2048]{2,0,1:T(4,128)(2,1)} %bitcast), calls=%async_computation | async-start | bytes 1048576 | tf_op jit(solution)/shard_map/all_to_all | solution.py:51
  117.6 27.7 %copy-start = (bf16[4,32,2048]{2,0,1:T(4,128)(2,1)}, bf16[4,32,2048]{2,0,1:T(4,128)(2,1)S(1)}, u32[]{:S(2)}) copy-start(bf16[4,32,2048]{2,0,1:T(4,128)(2,1)S(1)} %all-to-all-done) | copy-start | bytes 1572868
  227.1 3.4 copy-start.2
  227.1 3.4 copy-start.4
  369.8 2.2 copy-start.1
Sparse Core Ops, SparseCore 0:
  75.9 63.0 all-gather.6
  142.0 66.6 all-gather.4
where the time goes:
time: 429 us; the launch traced here: 426 us
  blocking collectives  133 us (31%)
  local copies, waits for them, and re-layouts  107 us (25%)
  waiting for transfers between devices  88.9 us (21%)
  matrix products  58.3 us (14%)
  other arithmetic  16.6 us (4%)
  between operations  13.6 us (3%)
  starting transfers between devices  7.62 us (2%)
    dot_general x12, matrix products, slot_term(): jnp.einsum('mbo,beo->mbe', obs_weight, gain_block, preferred_element_type...  58.3 us
    all_gather x1, waiting for transfers between devices, on_device(): lax.all_gather(obs_anom, 'region', axis=1, tiled=True)  56.9 us
    all_to_all x1, blocking collectives, on_device(): lax.all_to_all(updated, 'member', split_axis=0, concat_axis=1, tiled=True)  46.3 us
    all_gather x1, blocking collectives, on_device(): lax.all_gather(obs_model, 'member', axis=0, tiled=True)  38.7 us
    gather x12, local copies, waits for them, and re-layouts, slot_term(): obs_part = jnp.take(panel_anom, slot_ids, axis=1)  30.7 us
    gather x12, local copies, waits for them, and re-layouts, slot_term(): obs_weight = jnp.take(panel_weight, slot_ids, axis=1)  30.6 us
    all_gather x1, blocking collectives, on_device(): lax.all_gather(innovations, 'member', axis=0, tiled=True)  28.1 us
    all_gather x1, blocking collectives, on_device(): lax.all_gather(obs_coords.astype(jnp.bfloat16), 'region', axis=1, tiled=T...  20.3 us
  transfers between devices with their start and end apart: 3, of which 3 were waited for; matrix products, arithmetic and copies ran while one was open for 4% of the time, Pallas kernels for 0%

commit v1 on v0

v1 whole, which is shorter than its diff:
```python
import functools

import jax
import jax.numpy as jnp
from jax import lax
from jax.experimental import pallas as pl
from jax.experimental.pallas import tpu as pltpu
from jax.sharding import PartitionSpec as P

MESH = pl.DeviceIdType.MESH
F32 = jnp.float32
BF16 = jnp.bfloat16
TILE = 128
FEATS = 32
HALF_WIDTH = 0.6
CHUNKS = 4


def split3(v):
    first = v.astype(BF16).astype(F32)
    rest = v - first
    second = rest.astype(BF16).astype(F32)
    third = (rest - second).astype(BF16).astype(F32)
    return first, second, third


def pieces(coords):
    row = lax.broadcasted_iota(jnp.int32, coords.shape, 0)
    scaled = jnp.where(row < 3, (coords - 0.5) * (1.0 / HALF_WIDTH), 0.0)
    norm = jnp.sum(scaled * scaled, axis=0, keepdims=True)
    n1, n2, n3 = split3(norm)
    norms = jnp.where(row == 0, n1, jnp.where(row == 1, n2, jnp.where(row == 2, n3, 0.0)))
    ones = jnp.where(row < 3, 1.0, 0.0)
    return split3(scaled), norms, ones


def taper(square, scale):
    square = jnp.maximum(square, 1e-12)
    inverse = lax.rsqrt(square)
    z = square * inverse
    near = (
        ((-0.25 * scale * z + 0.5 * scale) * z + 0.625 * scale) * z - 5.0 / 3.0 * scale
    ) * square + scale
    edge = jnp.maximum(2.0 - z, 0.0)
    edge = edge * edge
    far = (edge * edge) * ((scale / 12.0) * z + (scale / 6.0) - (scale / 24.0) * inverse)
    return jnp.where(square <= 1.0, near, far)


def kernel(
    dims,
    sample,
    obs,
    innov,
    error,
    obs_coords,
    state_coords,
    neighbours,
    pattern,
    counts,
    out,
    mine,
    geo,
    gathered,
    gathered_geo,
    ring,
    geo_sel,
    arrived,
    fields,
    results,
    leaving,
    obs_rows,
    innov_rows,
    feat_rows,
    state_feats,
    panel_left,
    panel_weight,
    right,
    gains,
    xy_send,
    xy_recv,
    geo_send,
    geo_recv,
    up_send,
    up_recv,
    down_send,
    down_recv,
    sib_send,
    sib_recv,
    in_send,
    in_recv,
    in_own,
    out_send,
    out_recv,
):
    regions, devices = dims
    chips = devices // 2
    rows = sample.shape[0]
    members = rows * devices
    chunks, _, _, width = arrived.shape
    entries = chunks * width
    blocks = width // TILE
    slots = pattern.shape[1]
    panels = obs.shape[1] // TILE
    my_region = lax.axis_index("region")
    me = lax.axis_index("member")
    my_z = me // 2
    my_core = me % 2

    barrier = pltpu.get_barrier_semaphore()

    def greet_region(step, carry):
        peer = (my_region + step) % regions
        pl.semaphore_signal(barrier, inc=1, device_id=(peer, me), device_id_type=MESH)
        return carry

    def greet_member(step, carry):
        peer = (me + step) % devices
        pl.semaphore_signal(barrier, inc=1, device_id=(my_region, peer), device_id_type=MESH)
        return carry

    lax.fori_loop(1, regions, greet_region, 0)
    lax.fori_loop(1, devices, greet_member, 0)
    mine[0] = obs[...]
    mine[1] = innov[...]
    geo[0:3, :] = obs_coords[...]
    geo[3:4, :] = error[...]
    gathered[my_region] = mine[...]
    gathered_geo[my_region] = geo[...]
    pl.semaphore_wait(barrier, regions + devices - 2)

    def send_region(step, carry):
        peer = (my_region + step) % regions
        pltpu.make_async_remote_copy(
            src_ref=mine,
            dst_ref=gathered.at[my_region],
            send_sem=xy_send,
            recv_sem=xy_recv,
            device_id=(peer, me),
            device_id_type=MESH,
        ).start()
        pltpu.make_async_remote_copy(
            src_ref=geo,
            dst_ref=gathered_geo.at[my_region],
            send_sem=geo_send,
            recv_sem=geo_recv,
            device_id=(peer, me),
            device_id_type=MESH,
        ).start()
        return carry

    lax.fori_loop(1, regions, send_region, 0)

    def send_samples(chunk):
        def send(step, carry):
            peer = (me + step) % devices
            begin = pl.multiple_of(peer * entries + chunk * width, TILE)
            pltpu.make_async_remote_copy(
                src_ref=sample.at[:, pl.ds(begin, width)],
                dst_ref=arrived.at[chunk, me],
                send_sem=in_send,
                recv_sem=in_recv.at[chunk],
                device_id=(my_region, peer),
                device_id_type=MESH,
            ).start()
            return carry

        lax.fori_loop(1, devices, send, 0)
        begin = pl.multiple_of(me * entries + chunk * width, TILE)
        pltpu.make_async_copy(
            sample.at[:, pl.ds(begin, width)], arrived.at[chunk, me], in_own.at[chunk]
        ).start()

    send_samples(0)

    feat_rows[...] = jnp.zeros_like(feat_rows)
    panel_left[...] = jnp.zeros_like(panel_left)
    right[...] = jnp.zeros_like(right)
    state4 = jnp.concatenate([state_coords[...], jnp.zeros((1, entries), F32)], axis=0)
    (s1, s2, s3), norms, ones = pieces(state4)
    state_feats[...] = jnp.concatenate([s1, s1, s2, s2, s1, s3, norms, ones], axis=0).astype(BF16)

    pltpu.make_async_copy(gathered.at[0 : regions - 1], gathered.at[0 : regions - 1], xy_recv).wait()
    pltpu.make_async_copy(
        gathered_geo.at[0 : regions - 1], gathered_geo.at[0 : regions - 1], geo_recv
    ).wait()
    ring[me, 0] = gathered[my_region]
    geo_sel[0] = gathered_geo[my_region]
    for which in range(2):
        chosen = neighbours[0, which]
        ring[me, which + 1] = gathered[chosen]
        geo_sel[which + 1] = gathered_geo[chosen]

    def around(source_z, target_z, send_sem, recv_sem):
        source = source_z * 2 + my_core
        return pltpu.make_async_remote_copy(
            src_ref=ring.at[source],
            dst_ref=ring.at[source],
            send_sem=send_sem,
            recv_sem=recv_sem,
            device_id=(my_region, target_z * 2 + my_core),
            device_id_type=MESH,
        )

    def to_sibling(source_z):
        source = source_z * 2 + my_core
        pltpu.make_async_remote_copy(
            src_ref=ring.at[source],
            dst_ref=ring.at[source],
            send_sem=sib_send,
            recv_sem=sib_recv,
            device_id=(my_region, my_z * 2 + 1 - my_core),
            device_id_type=MESH,
        ).start()

    above = (my_z + 1) % chips
    below = (my_z + chips - 1) % chips
    ups = chips // 2
    downs = chips - 1 - ups

    def up_copy(step):
        return around((my_z + chips - step) % chips, above, up_send, up_recv.at[step])

    def down_copy(step):
        return around((my_z + step) % chips, below, down_send, down_recv.at[step])

    up_copy(0).start()
    if downs > 0:
        down_copy(0).start()
    to_sibling(my_z)
    for step in range(ups):
        if step < chunks - 1:
            send_samples(step + 1)
        up_copy(step).wait_recv()
        if step + 1 < ups:
            up_copy(step + 1).start()
        to_sibling((my_z + chips - step - 1) % chips)
        if step < downs:
            down_copy(step).wait_recv()
            if step + 1 < downs:
                down_copy(step + 1).start()
            to_sibling((my_z + step + 1) % chips)
    for chunk in range(ups + 1, chunks):
        send_samples(chunk)
    pltpu.make_async_copy(ring.at[0:chips], ring.at[0:chips], sib_recv).wait()

    def prepare(which, carry):
        for source in range(devices):
            at = slice(source * rows, (source + 1) * rows)
            obs_rows[at, :] = ring[source, which, 0].astype(F32)
            innov_rows[at, :] = ring[source, which, 1].astype(F32)
        place = geo_sel[which]
        (y1, y2, y3), norms, ones = pieces(place)
        feat_rows[0:FEATS, :] = jnp.concatenate(
            [-2.0 * y1, -2.0 * y2, -2.0 * y1, -2.0 * y2, -2.0 * y3, -2.0 * y1, ones, norms], axis=0
        )
        for part in range(panels):
            lanes = slice(part * TILE, (part + 1) * TILE)
            model = obs_rows[:, lanes]
            deviation = model - jnp.sum(model, axis=0, keepdims=True) / members
            spread = (
                jnp.sum(deviation * deviation, axis=0, keepdims=True) / (members - 1)
                + place[3:4, lanes]
            )
            panel = which * panels + part
            panel_left[panel, :, 0:members] = deviation.T.astype(BF16)
            panel_left[panel, :, TILE:] = feat_rows[:, lanes].T.astype(BF16)
            panel_weight[panel] = (innov_rows[:, lanes] * (1.0 / spread)).astype(BF16)
        return carry

    lax.fori_loop(0, 3, prepare, 0)

    scale = 1.0 / (members - 1)

    def analyse_chunk(chunk, carry):
        pltpu.make_async_copy(
            arrived.at[chunk, 0 : devices - 1], arrived.at[chunk, 0 : devices - 1], in_recv.at[chunk]
        ).wait()
        pltpu.make_async_copy(arrived.at[chunk, 0], arrived.at[chunk, 0], in_own.at[chunk]).wait()
        for source in range(devices):
            fields[source * rows : (source + 1) * rows, :] = arrived[chunk, source].astype(F32)

        def analyse_block(block, carry):
            index = chunk * blocks + block
            lanes = pl.ds(pl.multiple_of(block * TILE, TILE), TILE)
            value = fields[:, lanes]
            centre = jnp.sum(value, axis=0, keepdims=True) / members
            right[0:members, 0:TILE] = (value - centre).astype(BF16)
            right[TILE : TILE + FEATS, TILE:] = state_feats[
                :, pl.ds(pl.multiple_of(index * TILE, TILE), TILE)
            ]
            total = value
            live = counts[0, index]
            for pair in range(slots // 2):
                weights = []
                for half in range(2):
                    slot = 2 * pair + half
                    panel = pattern[index, slot]
                    both = jnp.dot(panel_left[panel], right[...], preferred_element_type=F32)
                    gain = taper(both[:, TILE:], scale) * both[:, 0:TILE]
                    gains[half * TILE : (half + 1) * TILE, :] = gain.astype(BF16)
                    mask = jnp.where(slot < live, 1.0, 0.0).astype(F32)
                    weights.append(panel_weight[panel] * jnp.full((members, TILE), mask, F32).astype(BF16))
                total = total + jnp.dot(
                    jnp.concatenate(weights, axis=1), gains[...], preferred_element_type=F32
                )
            results[:, lanes] = total
            return carry

        lax.fori_loop(0, blocks, analyse_block, 0)
        for target in range(devices):
            leaving[chunk, target] = results[target * rows : (target + 1) * rows, :].astype(BF16)
        begin = pl.multiple_of(me * entries + chunk * width, TILE)

        def send_back(step, carry):
            peer = (me + step) % devices
            pltpu.make_async_remote_copy(
                src_ref=leaving.at[chunk, peer],
                dst_ref=out.at[:, pl.ds(begin, width)],
                send_sem=out_send,
                recv_sem=out_recv,
                device_id=(my_region, peer),
                device_id_type=MESH,
            ).start()
            return carry

        lax.fori_loop(1, devices, send_back, 0)
        pltpu.make_async_copy(
            leaving.at[chunk, me], out.at[:, pl.ds(begin, width)], in_own.at[chunk]
        ).start()
        return carry

    lax.fori_loop(0, chunks, analyse_chunk, 0)

    for chunk in range(chunks):
        pltpu.make_async_copy(leaving.at[chunk, 0], leaving.at[chunk, 0], in_own.at[chunk]).wait()
    others = leaving.at[:, 0 : devices - 1]
    pltpu.make_async_copy(others, others, out_recv).wait()
    pltpu.make_async_copy(others, others, out_send).wait()
    pltpu.make_async_copy(others, others, in_send).wait()
    pltpu.make_async_copy(gathered.at[0 : regions - 1], gathered.at[0 : regions - 1], xy_send).wait()
    pltpu.make_async_copy(
        gathered_geo.at[0 : regions - 1], gathered_geo.at[0 : regions - 1], geo_send
    ).wait()
    pltpu.make_async_copy(ring.at[0:ups], ring.at[0:ups], up_send).wait()
    if downs > 0:
        pltpu.make_async_copy(ring.at[0:downs], ring.at[0:downs], down_send).wait()
    pltpu.make_async_copy(ring.at[0:chips], ring.at[0:chips], sib_send).wait()


def on_device(
    regions,
    devices,
    sample_matrix,
    state_coords,
    obs_model,
    innovations,
    obs_error,
    obs_coords,
    neighbours,
    pattern,
    counts,
):
    rows = sample_matrix.shape[0]
    obs_count = obs_model.shape[1]
    entries = state_coords.shape[1]
    width = entries // CHUNKS
    members = rows * devices
    panels = 3 * obs_count // TILE
    chips = devices // 2
    vmem = pl.BlockSpec(memory_space=pltpu.VMEM)
    smem = pl.BlockSpec(memory_space=pltpu.SMEM)
    anywhere = pl.BlockSpec(memory_space=pl.ANY)
    dma = pltpu.SemaphoreType.DMA
    return pl.pallas_call(
        functools.partial(kernel, (regions, devices)),
        out_shape=jax.ShapeDtypeStruct(sample_matrix.shape, sample_matrix.dtype),
        in_specs=[anywhere, vmem, vmem, vmem, vmem, vmem, smem, smem, smem],
        out_specs=anywhere,
        scratch_shapes=[
            pltpu.VMEM((2, rows, obs_count), BF16),
            pltpu.VMEM((4, obs_count), F32),
            pltpu.VMEM((regions, 2, rows, obs_count), BF16),
            pltpu.VMEM((regions, 4, obs_count), F32),
            pltpu.VMEM((devices, 3, 2, rows, obs_count), BF16),
            pltpu.VMEM((3, 4, obs_count), F32),
            pltpu.VMEM((CHUNKS, devices, rows, width), BF16),
            pltpu.VMEM((members, width), F32),
            pltpu.VMEM((members, width), F32),
            pltpu.VMEM((CHUNKS, devices, rows, width), BF16),
            pltpu.VMEM((members, obs_count), F32),
            pltpu.VMEM((members, obs_count), F32),
            pltpu.VMEM((TILE, obs_count), F32),
            pltpu.VMEM((FEATS, entries), BF16),
            pltpu.VMEM((panels, TILE, 2 * TILE), BF16),
            pltpu.VMEM((panels, members, TILE), BF16),
            pltpu.VMEM((2 * TILE, 2 * TILE), BF16),
            pltpu.VMEM((2 * TILE, TILE), BF16),
            dma,
            dma,
            dma,
            dma,
            dma,
            dma((chips,)),
            dma,
            dma((chips,)),
            dma,
            dma,
            dma,
            dma((CHUNKS,)),
            dma((CHUNKS,)),
            dma,
            dma,
        ],
        compiler_params=pltpu.CompilerParams(
            collective_id=0, has_side_effects=True, vmem_limit_bytes=48 * 2**20
        ),
    )(
        sample_matrix,
        obs_model,
        innovations,
        obs_error.reshape(1, -1),
        obs_coords,
        state_coords,
        neighbours,
        pattern,
        counts.reshape(1, -1),
    )


def solution(mesh):
    in_specs = (
        P("member", "region"),
        P(None, ("region", "member")),
        P("member", "region"),
        P("member", "region"),
        P("region"),
        P(None, "region"),
        P("region", None),
        P(("region", "member"), None),
        P(("region", "member")),
    )
    return jax.shard_map(
        functools.partial(on_device, mesh.shape["region"], mesh.shape["member"]),
        mesh=mesh,
        in_specs=in_specs,
        out_specs=P("member", "region"),
        check_vma=False,
    )
```

time: 429 us -> 110 us (0.26)
  blocking collectives: 133 us -> 0 us
  Pallas kernels: 0 us -> 103 us
  local copies, waits for them, and re-layouts: 107 us -> 6.76 us
  waiting for transfers between devices: 88.9 us -> 0 us
  matrix products: 58.3 us -> 0 us
  other arithmetic: 16.6 us -> 0 us
  between operations: 13.6 us -> 0.02 us
  starting transfers between devices: 7.62 us -> 0 us
    pallas_call x0 -> x1, Pallas kernels: none -> 103 us  [on_device(): pl.pallas_call(functools.partial(kernel, (regions, devices)), out_shape=j...]
    all_gather x3 -> x0, blocking collectives: 87 us -> none  [the longest x1 38.7 us: on_device(): lax.all_gather(obs_model, 'member', axis=0, tiled=True)]
    all_gather x2 -> x0, waiting for transfers between devices: 76.2 us -> none  [the longest x1 56.9 us: on_device(): lax.all_gather(obs_anom, 'region', axis=1, tiled=True)]
    gather x39 -> x0, local copies, waits for them, and re-layouts: 74.5 us -> none  [the longest x12 30.7 us: slot_term(): obs_part = jnp.take(panel_anom, slot_ids, axis=1)]
    dot_general x12 -> x0, matrix products: 58.3 us -> none  [slot_term(): jnp.einsum('mbo,beo->mbe', obs_weight, gain_block, preferred_element_type...]
    all_to_all x1 -> x0, blocking collectives: 46.3 us -> none  [on_device(): lax.all_to_all(updated, 'member', split_axis=0, concat_axis=1, tiled=True)]
    reshape x3 -> x0, local copies, waits for them, and re-layouts: 13.2 us -> none  [the longest x2 12.8 us: pick_regions(): split = array.reshape(leading, regions_all, -1)]
    all_gather x2 -> x0, local copies, waits for them, and re-layouts: 12.8 us -> none  [the longest x1 6.38 us: on_device(): lax.all_gather(weighted, 'region', axis=1, tiled=True)]
  transfers between devices with their start and end apart: 3 -> 0, of which waited for: 3 -> 0; matrix products, arithmetic and copies ran while one was open for 4% -> 0% of each run, Pallas kernels for 0% -> 0%
where the time goes in v1:
time: 110 us
  Pallas kernels  103 us (94%)
  local copies, waits for them, and re-layouts  6.76 us (6%)
    pallas_call x1, Pallas kernels, on_device(): pl.pallas_call(functools.partial(kernel, (regions, devices)), out_shape=j...  103 us
    unnamed x19, local copies, waits for them, and re-layouts  6.76 us

profile of v1, /device:TPU:1, one launch (start us, length us, event | category | flops | bytes accessed | tf_op | source)
XLA Modules:
  0.0 109.6 jit_solution(5969605124583325189)
XLA Ops:
  0.0 0.0 copy-start.7
  0.0 0.0 copy-start.8
  0.0 0.7 copy-done.7
  0.7 0.0 copy-done.8
  0.7 0.0 copy-start
  0.7 1.0 copy-done
  1.7 0.0 copy-start.1
  1.7 0.8 copy-done.1
  2.5 0.0 copy-start.2
  2.5 0.7 copy-done.2
  3.2 0.0 copy-start.3
  3.2 0.7 copy-done.3
  3.9 0.0 copy-start.4
  3.9 0.7 copy-done.4
  4.6 0.0 copy-start.5
  4.6 0.7 copy-done.5
  5.3 0.0 copy-start.6
  5.3 0.7 copy-done.6
  6.0 102.8 %shard_map.91 = bf16[4,65536]{1,0:T(4,128)(2,1)S(1)} custom-call(bf16[4,65536]{1,0:T(4,128)(2,1)S(1)} %copy-done, bf16[4,1024]{1,0:T(4,128)(2,1)S(1)} %copy-done.3, bf16[4,1024]{1,0:T(4,128)(2,1)S(1)} %copy-done.4, f32[1,1024]{1,0:T(1,128)S(1)} %bitcast.2, f32[3,1024]{1,0:T(4,128)S(1)} %copy-done.2, f32[3,2048]{1,0:T(4,128)S(1)} %copy-done.1, ...), custom_call_target="tpu_custom_call" | custom-call | tf_op jit(solution)/shard_map/pallas_call | solution.py:375
  108.8 0.8 copy.11
Async XLA Ops:
  0.0 0.7 copy-start.7
  0.0 0.7 copy-start.8
  0.7 1.0 copy-start
  1.7 0.8 copy-start.1
  2.5 0.7 copy-start.2
  3.2 0.7 copy-start.3
  3.9 0.7 copy-start.4
  4.6 0.7 copy-start.5
  5.3 0.7 copy-start.6

commit v2 on v1

--- a/solution.py
+++ b/solution.py
@@ -13,7 +13,14 @@
 TILE = 128
 FEATS = 32
 HALF_WIDTH = 0.6
-CHUNKS = 4
+CHUNKS = 8
+AHEAD = 2
+EARLY = 2
+STRIDE = 2
+
+
+def wrap(index, size):
+    return jnp.where(index >= size, index - size, index)
 
 
 def split3(v):
@@ -50,15 +57,22 @@
 def kernel(
     dims,
     sample,
-    obs,
-    innov,
+    obs_in,
+    innov_in,
+    error_in,
+    obs_coords_in,
+    state_coords_in,
+    neighbours_in,
+    pattern_in,
+    counts_in,
+    out,
     error,
     obs_coords,
     state_coords,
     neighbours,
     pattern,
     counts,
-    out,
+    load_sem,
     mine,
     geo,
     gathered,
@@ -66,7 +80,8 @@
     ring,
     geo_sel,
     arrived,
-    fields,
+    field_a,
+    field_b,
     results,
     leaving,
     obs_rows,
@@ -75,8 +90,10 @@
     state_feats,
     panel_left,
     panel_weight,
-    right,
-    gains,
+    right_a,
+    right_b,
+    product_a,
+    product_b,
     xy_send,
     xy_recv,
     geo_send,
@@ -101,59 +118,74 @@
     entries = chunks * width
     blocks = width // TILE
     slots = pattern.shape[1]
-    panels = obs.shape[1] // TILE
+    panels = obs_in.shape[1] // TILE
     my_region = lax.axis_index("region")
     me = lax.axis_index("member")
     my_z = me // 2
     my_core = me % 2
 
+    loads = [
+        pltpu.make_async_copy(source, target, load_sem.at[index])
+        for index, (source, target) in enumerate(
+            (
+                (obs_in, mine.at[0]),
+                (innov_in, mine.at[1]),
+                (error_in, error),
+                (obs_coords_in, obs_coords),
+                (state_coords_in, state_coords),
+                (neighbours_in, neighbours),
+                (pattern_in, pattern),
+                (counts_in, counts),
+            )
+        )
+    ]
+    for load in loads:
+        load.start()
     barrier = pltpu.get_barrier_semaphore()
 
     def greet_region(step, carry):
-        peer = (my_region + step) % regions
+        peer = wrap(my_region + step, regions)
         pl.semaphore_signal(barrier, inc=1, device_id=(peer, me), device_id_type=MESH)
         return carry
 
     def greet_member(step, carry):
-        peer = (me + step) % devices
+        peer = wrap(me + step, devices)
         pl.semaphore_signal(barrier, inc=1, device_id=(my_region, peer), device_id_type=MESH)
         return carry
 
     lax.fori_loop(1, regions, greet_region, 0)
     lax.fori_loop(1, devices, greet_member, 0)
-    mine[0] = obs[...]
-    mine[1] = innov[...]
+    for load in loads:
+        load.wait()
     geo[0:3, :] = obs_coords[...]
     geo[3:4, :] = error[...]
-    gathered[my_region] = mine[...]
-    gathered_geo[my_region] = geo[...]
     pl.semaphore_wait(barrier, regions + devices - 2)
 
-    def send_region(step, carry):
-        peer = (my_region + step) % regions
+    def send_obs(step, carry):
         pltpu.make_async_remote_copy(
             src_ref=mine,
             dst_ref=gathered.at[my_region],
             send_sem=xy_send,
             recv_sem=xy_recv,
-            device_id=(peer, me),
+            device_id=(wrap(my_region + step, regions), me),
             device_id_type=MESH,
         ).start()
+        return carry
+
+    def send_geo(step, carry):
         pltpu.make_async_remote_copy(
             src_ref=geo,
             dst_ref=gathered_geo.at[my_region],
             send_sem=geo_send,
             recv_sem=geo_recv,
-            device_id=(peer, me),
+            device_id=(wrap(my_region + step, regions), me),
             device_id_type=MESH,
         ).start()
         return carry
 
-    lax.fori_loop(1, regions, send_region, 0)
-
     def send_samples(chunk):
         def send(step, carry):
-            peer = (me + step) % devices
+            peer = wrap(me + step, devices)
             begin = pl.multiple_of(peer * entries + chunk * width, TILE)
             pltpu.make_async_remote_copy(
                 src_ref=sample.at[:, pl.ds(begin, width)],
@@ -171,77 +203,91 @@
             sample.at[:, pl.ds(begin, width)], arrived.at[chunk, me], in_own.at[chunk]
         ).start()
 
-    send_samples(0)
-
-    feat_rows[...] = jnp.zeros_like(feat_rows)
-    panel_left[...] = jnp.zeros_like(panel_left)
-    right[...] = jnp.zeros_like(right)
-    state4 = jnp.concatenate([state_coords[...], jnp.zeros((1, entries), F32)], axis=0)
-    (s1, s2, s3), norms, ones = pieces(state4)
-    state_feats[...] = jnp.concatenate([s1, s1, s2, s2, s1, s3, norms, ones], axis=0).astype(BF16)
-
-    pltpu.make_async_copy(gathered.at[0 : regions - 1], gathered.at[0 : regions - 1], xy_recv).wait()
-    pltpu.make_async_copy(
-        gathered_geo.at[0 : regions - 1], gathered_geo.at[0 : regions - 1], geo_recv
-    ).wait()
-    ring[me, 0] = gathered[my_region]
-    geo_sel[0] = gathered_geo[my_region]
-    for which in range(2):
-        chosen = neighbours[0, which]
-        ring[me, which + 1] = gathered[chosen]
-        geo_sel[which + 1] = gathered_geo[chosen]
-
-    def around(source_z, target_z, send_sem, recv_sem):
-        source = source_z * 2 + my_core
+    def around(piece, source_z, target_z, send_sem, recv_sem):
+        source = wrap(source_z, chips) * 2 + my_core
         return pltpu.make_async_remote_copy(
-            src_ref=ring.at[source],
-            dst_ref=ring.at[source],
+            src_ref=ring.at[source, piece],
+            dst_ref=ring.at[source, piece],
             send_sem=send_sem,
             recv_sem=recv_sem,
-            device_id=(my_region, target_z * 2 + my_core),
+            device_id=(my_region, wrap(target_z, chips) * 2 + my_core),
             device_id_type=MESH,
         )
 
-    def to_sibling(source_z):
-        source = source_z * 2 + my_core
+    def to_sibling(piece, source_z):
+        source = wrap(source_z, chips) * 2 + my_core
         pltpu.make_async_remote_copy(
-            src_ref=ring.at[source],
-            dst_ref=ring.at[source],
+            src_ref=ring.at[source, piece],
+            dst_ref=ring.at[source, piece],
             send_sem=sib_send,
             recv_sem=sib_recv,
             device_id=(my_region, my_z * 2 + 1 - my_core),
             device_id_type=MESH,
         ).start()
 
-    above = (my_z + 1) % chips
-    below = (my_z + chips - 1) % chips
     ups = chips // 2
     downs = chips - 1 - ups
 
-    def up_copy(step):
-        return around((my_z + chips - step) % chips, above, up_send, up_recv.at[step])
-
-    def down_copy(step):
-        return around((my_z + step) % chips, below, down_send, down_recv.at[step])
-
-    up_copy(0).start()
-    if downs > 0:
-        down_copy(0).start()
-    to_sibling(my_z)
+    def up_copy(piece, step):
+        return around(piece, my_z + chips - step, my_z + 1, up_send, up_recv.at[piece, step])
+
+    def down_copy(piece, step):
+        return around(piece, my_z + step, my_z + chips - 1, down_send, down_recv.at[piece, step])
+
+    def launch(piece):
+        up_copy(piece, 0).start()
+        if downs > 0:
+            down_copy(piece, 0).start()
+        to_sibling(piece, my_z)
+
+    def forward(piece, step):
+        up_copy(piece, step).wait_recv()
+        if step + 1 < ups:
+            up_copy(piece, step + 1).start()
+        to_sibling(piece, my_z + chips - step - 1)
+        if step < downs:
+            down_copy(piece, step).wait_recv()
+            if step + 1 < downs:
+                down_copy(piece, step + 1).start()
+            to_sibling(piece, my_z + step + 1)
+
+    ring[me, 0] = mine[...]
+    launch(0)
+    lax.fori_loop(1, regions, send_obs, 0)
+    for chunk in range(min(EARLY, chunks)):
+        send_samples(chunk)
+
+    feat_rows[...] = jnp.zeros_like(feat_rows)
+    panel_left[...] = jnp.zeros_like(panel_left)
+    right_a[...] = jnp.zeros_like(right_a)
+    right_b[...] = jnp.zeros_like(right_b)
+    state4 = jnp.concatenate([state_coords[...], jnp.zeros((1, entries), F32)], axis=0)
+    (s1, s2, s3), norms, ones = pieces(state4)
+    state_feats[...] = jnp.concatenate([s1, s1, s2, s2, s1, s3, norms, ones], axis=0).astype(BF16)
+
+    ahead = min(AHEAD, ups)
+    for step in range(ahead):
+        forward(0, step)
+    pltpu.make_async_copy(gathered.at[0 : regions - 1], gathered.at[0 : regions - 1], xy_recv).wait()
+    for which in range(2):
+        ring[me, which + 1] = gathered[neighbours[0, which]]
+        launch(which + 1)
+    lax.fori_loop(1, regions, send_geo, 0)
     for step in range(ups):
-        if step < chunks - 1:
-            send_samples(step + 1)
-        up_copy(step).wait_recv()
-        if step + 1 < ups:
-            up_copy(step + 1).start()
-        to_sibling((my_z + chips - step - 1) % chips)
-        if step < downs:
-            down_copy(step).wait_recv()
-            if step + 1 < downs:
-                down_copy(step + 1).start()
-            to_sibling((my_z + step + 1) % chips)
-    for chunk in range(ups + 1, chunks):
+        if step + ahead < ups:
+            forward(0, step + ahead)
+        forward(1, step)
+        forward(2, step)
+        if step % STRIDE == 0 and EARLY + step // STRIDE < chunks:
+            send_samples(EARLY + step // STRIDE)
+    for chunk in range(EARLY + (ups + STRIDE - 1) // STRIDE, chunks):
         send_samples(chunk)
+    pltpu.make_async_copy(
+        gathered_geo.at[0 : regions - 1], gathered_geo.at[0 : regions - 1], geo_recv
+    ).wait()
+    geo_sel[0] = geo[...]
+    for which in range(2):
+        geo_sel[which + 1] = gathered_geo[neighbours[0, which]]
     pltpu.make_async_copy(ring.at[0:chips], ring.at[0:chips], sib_recv).wait()
 
     def prepare(which, carry):
@@ -272,48 +318,67 @@
 
     scale = 1.0 / (members - 1)
 
-    def analyse_chunk(chunk, carry):
+    def await_chunk(chunk):
         pltpu.make_async_copy(
             arrived.at[chunk, 0 : devices - 1], arrived.at[chunk, 0 : devices - 1], in_recv.at[chunk]
         ).wait()
         pltpu.make_async_copy(arrived.at[chunk, 0], arrived.at[chunk, 0], in_own.at[chunk]).wait()
+
+    def products(chunk, block, field, right, product):
+        index = chunk * blocks + block
+        lanes = slice(block * TILE, (block + 1) * TILE)
         for source in range(devices):
-            fields[source * rows : (source + 1) * rows, :] = arrived[chunk, source].astype(F32)
-
-        def analyse_block(block, carry):
-            index = chunk * blocks + block
-            lanes = pl.ds(pl.multiple_of(block * TILE, TILE), TILE)
-            value = fields[:, lanes]
-            centre = jnp.sum(value, axis=0, keepdims=True) / members
-            right[0:members, 0:TILE] = (value - centre).astype(BF16)
-            right[TILE : TILE + FEATS, TILE:] = state_feats[
-                :, pl.ds(pl.multiple_of(index * TILE, TILE), TILE)
-            ]
-            total = value
-            live = counts[0, index]
-            for pair in range(slots // 2):
-                weights = []
-                for half in range(2):
-                    slot = 2 * pair + half
-                    panel = pattern[index, slot]
-                    both = jnp.dot(panel_left[panel], right[...], preferred_element_type=F32)
-                    gain = taper(both[:, TILE:], scale) * both[:, 0:TILE]
-                    gains[half * TILE : (half + 1) * TILE, :] = gain.astype(BF16)
-                    mask = jnp.where(slot < live, 1.0, 0.0).astype(F32)
-                    weights.append(panel_weight[panel] * jnp.full((members, TILE), mask, F32).astype(BF16))
-                total = total + jnp.dot(
-                    jnp.concatenate(weights, axis=1), gains[...], preferred_element_type=F32
-                )
-            results[:, lanes] = total
-            return carry
-
-        lax.fori_loop(0, blocks, analyse_block, 0)
+            field[source * rows : (source + 1) * rows, :] = arrived[chunk, source, :, lanes].astype(F32)
+        value = field[...]
+        centre = jnp.sum(value, axis=0, keepdims=True) / members
+        right[0:members, 0:TILE] = (value - centre).astype(BF16)
+        right[TILE : TILE + FEATS, TILE:] = state_feats[
+            :, pl.ds(pl.multiple_of(index * TILE, TILE), TILE)
+        ]
+        left = jnp.concatenate([panel_left[pattern[index, slot]] for slot in range(slots)], axis=0)
+        product[...] = jnp.dot(left, right[...], preferred_element_type=F32)
+
+    def update(chunk, block, field, product):
+        index = chunk * blocks + block
+        live = counts[0, index]
+        gains, weights = [], []
+        for slot in range(slots):
+            at = slice(slot * TILE, (slot + 1) * TILE)
+            gains.append((taper(product[at, TILE:], scale) * product[at, 0:TILE]).astype(BF16))
+            mask = jnp.where(slot < live, 1.0, 0.0).astype(F32)
+            weights.append(
+                panel_weight[pattern[index, slot]] * jnp.full((members, TILE), mask, F32).astype(BF16)
+            )
+        results[:, block * TILE : (block + 1) * TILE] = field[...] + jnp.dot(
+            jnp.concatenate(weights, axis=1),
+            jnp.concatenate(gains, axis=0),
+            preferred_element_type=F32,
+        )
+
+    await_chunk(0)
+    products(0, 0, field_a, right_a, product_a)
+
+    def analyse_chunk(chunk, carry):
+        for block in range(0, blocks, 2):
+            products(chunk, block + 1, field_b, right_b, product_b)
+            update(chunk, block, field_a, product_a)
+            if block + 2 < blocks:
+                products(chunk, block + 2, field_a, right_a, product_a)
+            else:
+
+                @pl.when(chunk + 1 < chunks)
+                def _():
+                    await_chunk(chunk + 1)
+
+                coming = jnp.minimum(chunk + 1, chunks - 1)
+                products(coming, 0, field_a, right_a, product_a)
+            update(chunk, block + 1, field_b, product_b)
         for target in range(devices):
             leaving[chunk, target] = results[target * rows : (target + 1) * rows, :].astype(BF16)
         begin = pl.multiple_of(me * entries + chunk * width, TILE)
 
         def send_back(step, carry):
-            peer = (me + step) % devices
+            peer = wrap(me + step, devices)
             pltpu.make_async_remote_copy(
                 src_ref=leaving.at[chunk, peer],
                 dst_ref=out.at[:, pl.ds(begin, width)],
@@ -367,17 +432,23 @@
     width = entries // CHUNKS
     members = rows * devices
     panels = 3 * obs_count // TILE
+    slots = pattern.shape[1]
     chips = devices // 2
-    vmem = pl.BlockSpec(memory_space=pltpu.VMEM)
-    smem = pl.BlockSpec(memory_space=pltpu.SMEM)
-    anywhere = pl.BlockSpec(memory_space=pl.ANY)
+    hbm = pl.BlockSpec(memory_space=pltpu.HBM)
     dma = pltpu.SemaphoreType.DMA
     return pl.pallas_call(
         functools.partial(kernel, (regions, devices)),
         out_shape=jax.ShapeDtypeStruct(sample_matrix.shape, sample_matrix.dtype),
-        in_specs=[anywhere, vmem, vmem, vmem, vmem, vmem, smem, smem, smem],
-        out_specs=anywhere,
+        in_specs=[hbm] * 9,
+        out_specs=hbm,
         scratch_shapes=[
+            pltpu.VMEM((1, obs_count), F32),
+            pltpu.VMEM(obs_coords.shape, F32),
+            pltpu.VMEM(state_coords.shape, F32),
+            pltpu.SMEM(neighbours.shape, jnp.int32),
+            pltpu.SMEM(pattern.shape, jnp.int32),
+            pltpu.SMEM((1, counts.shape[0]), jnp.int32),
+            dma((8,)),
             pltpu.VMEM((2, rows, obs_count), BF16),
             pltpu.VMEM((4, obs_count), F32),
             pltpu.VMEM((regions, 2, rows, obs_count), BF16),
@@ -385,7 +456,8 @@
             pltpu.VMEM((devices, 3, 2, rows, obs_count), BF16),
             pltpu.VMEM((3, 4, obs_count), F32),
             pltpu.VMEM((CHUNKS, devices, rows, width), BF16),
-            pltpu.VMEM((members, width), F32),
+            pltpu.VMEM((members, TILE), F32),
+            pltpu.VMEM((members, TILE), F32),
             pltpu.VMEM((members, width), F32),
             pltpu.VMEM((CHUNKS, devices, rows, width), BF16),
             pltpu.VMEM((members, obs_count), F32),
@@ -395,15 +467,17 @@
             pltpu.VMEM((panels, TILE, 2 * TILE), BF16),
             pltpu.VMEM((panels, members, TILE), BF16),
             pltpu.VMEM((2 * TILE, 2 * TILE), BF16),
-            pltpu.VMEM((2 * TILE, TILE), BF16),
-            dma,
-            dma,
-            dma,
-            dma,
-            dma,
-            dma((chips,)),
-            dma,
-            dma((chips,)),
+            pltpu.VMEM((2 * TILE, 2 * TILE), BF16),
+            pltpu.VMEM((slots * TILE, 2 * TILE), F32),
+            pltpu.VMEM((slots * TILE, 2 * TILE), F32),
+            dma,
+            dma,
+            dma,
+            dma,
+            dma,
+            dma((3, chips)),
+            dma,
+            dma((3, chips)),
             dma,
             dma,
             dma,
@@ -413,7 +487,7 @@
             dma,
         ],
         compiler_params=pltpu.CompilerParams(
-            collective_id=0, has_side_effects=True, vmem_limit_bytes=48 * 2**20
+            collective_id=0, has_side_effects=True, vmem_limit_bytes=60 * 2**20
         ),
     )(
         sample_matrix,

time: 110 us -> 87.4 us (0.79)
  Pallas kernels: 103 us -> 84.5 us
  local copies, waits for them, and re-layouts: 6.76 us -> 2.02 us
    pallas_call x1, Pallas kernels: 103 us -> 84.5 us  [on_device(): pl.pallas_call(functools.partial(kernel, (regions, devices)), out_shape=j...]
    unnamed x19 -> x1, local copies, waits for them, and re-layouts: 6.76 us -> 2.02 us
where the time goes in v2:
time: 87.4 us; the launch traced here: 86.5 us
  Pallas kernels  84.5 us (97%)
  local copies, waits for them, and re-layouts  2.02 us (2%)
    pallas_call x1, Pallas kernels, on_device(): pl.pallas_call(functools.partial(kernel, (regions, devices)), out_shape=j...  84.5 us
    unnamed x1, local copies, waits for them, and re-layouts  2.02 us

profile of v2, /device:TPU:1, one launch (start us, length us, event | category | flops | bytes accessed | tf_op | source)
XLA Modules:
  0.0 86.5 jit_solution(11451736527477922115)
XLA Ops:
  0.0 84.5 %shard_map.91 = bf16[4,65536]{1,0:T(4,128)(2,1)} custom-call(bf16[4,65536]{1,0:T(4,128)(2,1)} %sample.1, bf16[4,1024]{1,0:T(4,128)(2,1)} %obs_in.1, bf16[4,1024]{1,0:T(4,128)(2,1)} %innov_in.1, f32[1,1024]{1,0:T(1,128)} %bitcast.2, f32[3,1024]{1,0:T(4,128)} %obs_coords_in.1, f32[3,2048]{1,0:T(4,128)} %state_coords_in.1, s32[1,2]{1,0:T(1,128)} %neighbours_in.1, ...), custom_call_target="tpu_custom_call" | custom-call | tf_op jit(solution)/shard_map/pallas_call | solution.py:439
  84.5 2.0 %copy.11 = bf16[4,65536]{1,0:T(4,128)(2,1)} copy(bf16[4,65536]{1,0:T(4,128)(2,1)} %shard_map.91) | data formatting | bytes 1048576

commit v3 on v2

--- a/solution.py
+++ b/solution.py
@@ -14,9 +14,8 @@
 FEATS = 32
 HALF_WIDTH = 0.6
 CHUNKS = 8
-AHEAD = 2
-EARLY = 2
-STRIDE = 2
+SPREAD = (((0, 3), (0, 1)), ((3, 6), (3, 4), (1, 2)), ((6, 8), (6, 7), (4, 5)))
+SENT = (2, 1, 1, 1)
 
 
 def wrap(index, size):
@@ -203,59 +202,74 @@
             sample.at[:, pl.ds(begin, width)], arrived.at[chunk, me], in_own.at[chunk]
         ).start()
 
-    def around(piece, source_z, target_z, send_sem, recv_sem):
+    span = (slice(0, 1), slice(1, 3))
+    ups = chips // 2
+    downs = chips - 1 - ups
+
+    def hop(piece, source_z, target_z, send_sem, recv_sem):
         source = wrap(source_z, chips) * 2 + my_core
         return pltpu.make_async_remote_copy(
-            src_ref=ring.at[source, piece],
-            dst_ref=ring.at[source, piece],
+            src_ref=ring.at[source, span[piece]],
+            dst_ref=ring.at[source, span[piece]],
             send_sem=send_sem,
             recv_sem=recv_sem,
             device_id=(my_region, wrap(target_z, chips) * 2 + my_core),
             device_id_type=MESH,
         )
 
+    def up_copy(piece, done, goal):
+        return hop(
+            piece, my_z + chips - done, my_z + goal - done, up_send, up_recv.at[piece, goal - 1]
+        )
+
+    def down_copy(piece, done, goal):
+        return hop(
+            piece, my_z + done, my_z + chips - goal + done, down_send, down_recv.at[piece, goal - 1]
+        )
+
     def to_sibling(piece, source_z):
         source = wrap(source_z, chips) * 2 + my_core
         pltpu.make_async_remote_copy(
-            src_ref=ring.at[source, piece],
-            dst_ref=ring.at[source, piece],
+            src_ref=ring.at[source, span[piece]],
+            dst_ref=ring.at[source, span[piece]],
             send_sem=sib_send,
             recv_sem=sib_recv,
             device_id=(my_region, my_z * 2 + 1 - my_core),
             device_id_type=MESH,
         ).start()
 
-    ups = chips // 2
-    downs = chips - 1 - ups
-
-    def up_copy(piece, step):
-        return around(piece, my_z + chips - step, my_z + 1, up_send, up_recv.at[piece, step])
-
-    def down_copy(piece, step):
-        return around(piece, my_z + step, my_z + chips - 1, down_send, down_recv.at[piece, step])
+    def pass_on(piece, copy, reach, at):
+        for edges in SPREAD:
+            for done, goal in edges:
+                if done == at and goal <= reach:
+                    copy(piece, done, goal).start()
 
     def launch(piece):
-        up_copy(piece, 0).start()
-        if downs > 0:
-            down_copy(piece, 0).start()
+        pass_on(piece, up_copy, ups, 0)
+        pass_on(piece, down_copy, downs, 0)
         to_sibling(piece, my_z)
 
-    def forward(piece, step):
-        up_copy(piece, step).wait_recv()
-        if step + 1 < ups:
-            up_copy(piece, step + 1).start()
-        to_sibling(piece, my_z + chips - step - 1)
-        if step < downs:
-            down_copy(piece, step).wait_recv()
-            if step + 1 < downs:
-                down_copy(piece, step + 1).start()
-            to_sibling(piece, my_z + step + 1)
+    def forward(piece, round_at):
+        for done, goal in SPREAD[round_at]:
+            if goal <= ups:
+                up_copy(piece, done, goal).wait_recv()
+                pass_on(piece, up_copy, ups, goal)
+                to_sibling(piece, my_z + chips - goal)
+            if goal <= downs:
+                down_copy(piece, done, goal).wait_recv()
+                pass_on(piece, down_copy, downs, goal)
+                to_sibling(piece, my_z + goal)
 
     ring[me, 0] = mine[...]
     launch(0)
     lax.fori_loop(1, regions, send_obs, 0)
-    for chunk in range(min(EARLY, chunks)):
-        send_samples(chunk)
+    bounds = [min(sum(SENT[:count]), chunks) for count in range(len(SENT) + 1)] + [chunks]
+
+    def send_part(part):
+        for chunk in range(bounds[part], bounds[part + 1]):
+            send_samples(chunk)
+
+    send_part(0)
 
     feat_rows[...] = jnp.zeros_like(feat_rows)
     panel_left[...] = jnp.zeros_like(panel_left)
@@ -265,23 +279,21 @@
     (s1, s2, s3), norms, ones = pieces(state4)
     state_feats[...] = jnp.concatenate([s1, s1, s2, s2, s1, s3, norms, ones], axis=0).astype(BF16)
 
-    ahead = min(AHEAD, ups)
-    for step in range(ahead):
-        forward(0, step)
+    forward(0, 0)
     pltpu.make_async_copy(gathered.at[0 : regions - 1], gathered.at[0 : regions - 1], xy_recv).wait()
     for which in range(2):
         ring[me, which + 1] = gathered[neighbours[0, which]]
-        launch(which + 1)
+    launch(1)
     lax.fori_loop(1, regions, send_geo, 0)
-    for step in range(ups):
-        if step + ahead < ups:
-            forward(0, step + ahead)
-        forward(1, step)
-        forward(2, step)
-        if step % STRIDE == 0 and EARLY + step // STRIDE < chunks:
-            send_samples(EARLY + step // STRIDE)
-    for chunk in range(EARLY + (ups + STRIDE - 1) // STRIDE, chunks):
-        send_samples(chunk)
+    send_part(1)
+    forward(0, 1)
+    forward(1, 0)
+    send_part(2)
+    forward(0, 2)
+    forward(1, 1)
+    send_part(3)
+    forward(1, 2)
+    send_part(4)
     pltpu.make_async_copy(
         gathered_geo.at[0 : regions - 1], gathered_geo.at[0 : regions - 1], geo_recv
     ).wait()
@@ -475,9 +487,9 @@
             dma,
             dma,
             dma,
-            dma((3, chips)),
-            dma,
-            dma((3, chips)),
+            dma((2, chips)),
+            dma,
+            dma((2, chips)),
             dma,
             dma,
             dma,

time: 87.4 us -> 83.3 us (0.953)
  Pallas kernels: 84.5 us -> 81 us
    pallas_call x1, Pallas kernels: 84.5 us -> 81 us  [on_device(): pl.pallas_call(functools.partial(kernel, (regions, devices)), out_shape=j...]
where the time goes in v3:
time: 83.3 us; the launch traced here: 83 us
  Pallas kernels  81 us (97%)
  local copies, waits for them, and re-layouts  2.02 us (2%)
    pallas_call x1, Pallas kernels, on_device(): pl.pallas_call(functools.partial(kernel, (regions, devices)), out_shape=j...  81 us
    unnamed x1, local copies, waits for them, and re-layouts  2.02 us

profile of v3, /device:TPU:1, one launch (start us, length us, event | category | flops | bytes accessed | tf_op | source)
XLA Modules:
  0.0 83.0 jit_solution(7268458123742980709)
XLA Ops:
  0.0 81.0 %shard_map.91 = bf16[4,65536]{1,0:T(4,128)(2,1)} custom-call(bf16[4,65536]{1,0:T(4,128)(2,1)} %sample.1, bf16[4,1024]{1,0:T(4,128)(2,1)} %obs_in.1, bf16[4,1024]{1,0:T(4,128)(2,1)} %innov_in.1, f32[1,1024]{1,0:T(1,128)} %bitcast.2, f32[3,1024]{1,0:T(4,128)} %obs_coords_in.1, f32[3,2048]{1,0:T(4,128)} %state_coords_in.1, s32[1,2]{1,0:T(1,128)} %neighbours_in.1, ...), custom_call_target="tpu_custom_call" | custom-call | tf_op jit(solution)/shard_map/pallas_call | solution.py:451
  81.0 2.0 %copy.11 = bf16[4,65536]{1,0:T(4,128)(2,1)} copy(bf16[4,65536]{1,0:T(4,128)(2,1)} %shard_map.91) | data formatting | bytes 1048576

commit v4 on v3

--- a/solution.py
+++ b/solution.py
@@ -203,7 +203,7 @@
         ).start()
 
     span = (slice(0, 1), slice(1, 3))
-    ups = chips // 2
+    ups = (chips - 1) // 2
     downs = chips - 1 - ups
 
     def hop(piece, source_z, target_z, send_sem, recv_sem):

time: 83.3 us -> 81.5 us (0.978)
  Pallas kernels: 81 us -> 78.9 us
    pallas_call x1, Pallas kernels: 81 us -> 78.9 us  [on_device(): pl.pallas_call(functools.partial(kernel, (regions, devices)), out_shape=j...]
where the time goes in v4:
time: 81.5 us; the launch traced here: 80.9 us
  Pallas kernels  78.9 us (97%)
  local copies, waits for them, and re-layouts  2.02 us (2%)
    pallas_call x1, Pallas kernels, on_device(): pl.pallas_call(functools.partial(kernel, (regions, devices)), out_shape=j...  78.9 us
    unnamed x1, local copies, waits for them, and re-layouts  2.02 us

profile of v4, /device:TPU:1, one launch (start us, length us, event | category | flops | bytes accessed | tf_op | source)
XLA Modules:
  0.0 80.9 jit_solution(5063375235965989229)
XLA Ops:
  0.0 78.9 %shard_map.91 = bf16[4,65536]{1,0:T(4,128)(2,1)} custom-call(bf16[4,65536]{1,0:T(4,128)(2,1)} %sample.1, bf16[4,1024]{1,0:T(4,128)(2,1)} %obs_in.1, bf16[4,1024]{1,0:T(4,128)(2,1)} %innov_in.1, f32[1,1024]{1,0:T(1,128)} %bitcast.2, f32[3,1024]{1,0:T(4,128)} %obs_coords_in.1, f32[3,2048]{1,0:T(4,128)} %state_coords_in.1, s32[1,2]{1,0:T(1,128)} %neighbours_in.1, ...), custom_call_target="tpu_custom_call" | custom-call | tf_op jit(solution)/shard_map/pallas_call | solution.py:451
  78.9 2.0 %copy.11 = bf16[4,65536]{1,0:T(4,128)(2,1)} copy(bf16[4,65536]{1,0:T(4,128)(2,1)} %shard_map.91) | data formatting | bytes 1048576
